TPU v7x, 32 devices: a whole 2x2x4 slice. The times are simulated.
32 devices in a mesh: parts: 2 (over y), shard: 2 (over core), blk: 8 (over z, x).
Axes of the slice: x: 2, y: 2, z: 4, core: 2. Of those that a mesh axis runs over, the one named last changes fastest.
Arguments:
- queries_in: bfloat16 [4096, 1024], P(('parts', 'shard', 'blk')), parts along dimension 0, may hold values from -12 to 12
- query_weight: bfloat16 [1024, 1024], replicated, may hold values from -0.1875 to 0.1875
- bank: bfloat16 [2048, 1024], P(('parts', 'shard', 'blk')), parts along dimension 0, may hold values from -110 to 110
- uses: int32 [4096, 2], P(('parts', 'shard', 'blk')), parts along dimension 0, may hold values from 0 to 1, as said below
Outputs:
- retrieved: bfloat16 [4096, 1024], P(('parts', 'shard', 'blk')), parts along dimension 0
There are 2 independent parts, one for each index of `parts`. A program takes and returns all parts, laid end to end along the dimension named above; an argument that names none is the same for every part. Nothing has to cross between parts.
Inputs may be any that keep to these rules, and one draw needn't show every extreme that they name: `uses`: every query lists one or both of the two shards. Of the 128 queries of one device, at most 128 list one shard, and in every draw for every index of blk the queries of both devices at that index all list one same shard.
All inputs are finite; a program needn't handle non-finite values.
Results may differ from a plain program's by a relative error of at most 0.035.
Values may be sent and summed in bfloat16 or wider, within the bound.
A program may use at most 128 MiB of HBM per device.

v0:
```python
import math
import jax
import jax.numpy as jnp
from jax import lax
from jax.sharding import PartitionSpec as P

HEADS = 8
HEAD_DIM = 128
NEGATIVE = -1e30


def empty_carry(slot_count):
    return (
        jnp.full((slot_count, HEADS), NEGATIVE, jnp.float32),
        jnp.zeros((slot_count, HEADS), jnp.float32),
        jnp.zeros((slot_count, HEADS, HEAD_DIM), jnp.float32),
    )


def fold_piece(carry, query_heads, piece, allowed):
    slot_count = query_heads.shape[0]
    piece_rows = piece.shape[0]
    key_rows = math.gcd(piece_rows, 512)
    key_blocks = piece_rows // key_rows
    keys_blocked = piece.reshape(key_blocks, key_rows, HEADS, HEAD_DIM)
    mask_blocked = allowed.reshape(slot_count, key_blocks, key_rows).transpose(1, 0, 2)
    block_rows = math.gcd(slot_count, 128)
    blocks = slot_count // block_rows
    logit_scale = HEAD_DIM ** (-0.5)

    def blocked(array):
        return array.reshape((blocks, block_rows) + array.shape[1:])

    def key_step(state, inputs):
        keys_piece, mask_all = inputs

        def one_block(block_inputs):
            query_block, mask_block, top_old, total_old, accum_old = block_inputs
            scores = (
                jnp.einsum(
                    "shd,rhd->shr", query_block, keys_piece, preferred_element_type=jnp.float32
                )
                * logit_scale
            )
            scores = jnp.where(mask_block[:, None, :], scores, NEGATIVE)
            top_new = jnp.maximum(top_old, jnp.max(scores, axis=-1))
            weights = jnp.where(mask_block[:, None, :], jnp.exp(scores - top_new[..., None]), 0.0)
            factor = jnp.exp(top_old - top_new)
            total_new = total_old * factor + jnp.sum(weights, axis=-1)
            accum_new = accum_old * factor[..., None] + jnp.einsum(
                "shr,rhd->shd",
                weights.astype(jnp.bfloat16),
                keys_piece,
                preferred_element_type=jnp.float32,
            )
            return (top_new, total_new, accum_new)

        top_old, total_old, accum_old = state
        results = lax.map(
            one_block,
            (
                blocked(query_heads),
                blocked(mask_all),
                blocked(top_old),
                blocked(total_old),
                blocked(accum_old),
            ),
        )
        return (
            tuple((result.reshape((slot_count,) + result.shape[2:]) for result in results)),
            None,
        )

    final, unused = lax.scan(key_step, carry, (keys_blocked, mask_blocked))
    return final


def local(queries_in, query_weight, bank, uses):
    row_count = queries_in.shape[0]
    width_all = HEADS * HEAD_DIM
    projected = jnp.dot(queries_in, query_weight, preferred_element_type=jnp.float32).astype(
        jnp.bfloat16
    )
    positions = jnp.cumsum(uses, axis=0) - 1
    listed = uses > 0
    onehot_table = (positions.T[:, None, :] == jnp.arange(row_count)[None, :, None]) & listed.T[
        :, None, :
    ]
    outgoing = jnp.einsum(
        "sct,td->scd",
        onehot_table.astype(jnp.bfloat16),
        projected,
        preferred_element_type=jnp.float32,
    ).astype(jnp.bfloat16)
    incoming = lax.all_to_all(outgoing, "shard", split_axis=0, concat_axis=0, tiled=True)
    item_count = incoming.shape[1]
    slot_heads = incoming.reshape(2 * item_count, HEADS, HEAD_DIM)
    piece = lax.all_gather(bank, "blk", axis=0, tiled=True)
    allowed = jnp.ones((2 * item_count, piece.shape[0]), dtype=jnp.bool_)
    top_part, total_part, accum_part = fold_piece(
        empty_carry(2 * item_count), slot_heads, piece, allowed
    )
    accum_back = lax.all_to_all(
        accum_part.reshape(2, item_count, width_all).astype(jnp.bfloat16),
        "shard",
        split_axis=0,
        concat_axis=0,
        tiled=True,
    ).astype(jnp.float32)
    top_back = lax.all_to_all(
        top_part.reshape(2, item_count, HEADS).astype(jnp.bfloat16),
        "shard",
        split_axis=0,
        concat_axis=0,
        tiled=True,
    ).astype(jnp.float32)
    total_back = lax.all_to_all(
        total_part.reshape(2, item_count, HEADS).astype(jnp.bfloat16),
        "shard",
        split_axis=0,
        concat_axis=0,
        tiled=True,
    ).astype(jnp.float32)
    safe_slot = jnp.clip(positions, 0, row_count - 1)
    top_pair = jnp.stack(
        [jnp.take(top_back[member], safe_slot[:, member], axis=0) for member in range(2)], 1
    )
    total_pair = jnp.stack(
        [jnp.take(total_back[member], safe_slot[:, member], axis=0) for member in range(2)], 1
    )
    accum_pair = jnp.stack(
        [jnp.take(accum_back[member], safe_slot[:, member], axis=0) for member in range(2)], 1
    )
    accum_pair = accum_pair.reshape(row_count, 2, HEADS, HEAD_DIM)
    top_pair = jnp.where(listed[:, :, None], top_pair, NEGATIVE)
    highest = jnp.max(top_pair, axis=1)
    scale_pair = jnp.where(listed[:, :, None], jnp.exp(top_pair - highest[:, None, :]), 0.0)
    total_all = jnp.sum(scale_pair * total_pair, axis=1)
    accum_all = jnp.sum(scale_pair[..., None] * accum_pair, axis=1)
    return (accum_all / total_all[..., None]).reshape(row_count, width_all).astype(jnp.bfloat16)


def solution(mesh):
    in_specs = (
        P(("parts", "shard", "blk"), None),
        P(),
        P(("parts", "shard", "blk"), None),
        P(("parts", "shard", "blk"), None),
    )
    out_specs = P(("parts", "shard", "blk"), None)
    return jax.shard_map(local, mesh=mesh, in_specs=in_specs, out_specs=out_specs, check_vma=False)
```

profile of v0, /device:TPU:1, one launch (start us, length us, event | category | flops | bytes accessed | tf_op | source)
XLA Modules:
  0.0 94.7 jit_solution(11347580435513448345)
XLA Ops:
  6.5 0.0 copy-start
  6.5 0.0 all-gather.2.cloned.1.call-start
  6.5 0.7 all-gather.2.cloned.1.call-update
  7.3 0.8 copy.41
  8.1 0.1 copy.45
  8.1 0.2 reduce_window_sum.11
  8.3 0.1 copy.44
  8.4 0.0 copy-done
  8.4 2.4 %convolution_convert_fusion = bf16[2,128,1024]{2,1,0:T(8,128)(2,1)} fusion(bf16[128,1024]{1,0:T(8,128)(2,1)} %param.10, bf16[1024,1024]{1,0:T(8,128)(2,1)S(1)} %copy-done, s32[2,128]{1,0:T(2,128)S(1)} %copy.44, pred[2,128]{1,0:T(4,128)(4,1)S(1)} %copy.45), kind=kOutput, calls=%fused_computation.29 | convolution fusion | flops 336003072 | bytes 2884864 | tf_op jit(solution)/shard_map/sct,td->scd/dot_general | solution.py:89
  10.8 3.5 %all-to-all-start = ((bf16[2,128,1024]{2,1,0:T(8,128)(2,1)}), bf16[2,128,1024]{2,1,0:T(8,128)(2,1)S(1)}, u32[]{:S(2)}, u32[]{:S(2)}) async-start(bf16[2,128,1024]{2,1,0:T(8,128)(2,1)} %convolution_convert_fusion), calls=%async_computation | async-start | bytes 1048576 | tf_op jit(solution)/shard_map/all_to_all | solution.py:95
  14.4 0.1 copy.42
  14.5 1.3 %all-to-all-done = bf16[2,128,1024]{2,1,0:T(8,128)(2,1)S(1)} async-done(((bf16[2,128,1024]{2,1,0:T(8,128)(2,1)}), bf16[2,128,1024]{2,1,0:T(8,128)(2,1)S(1)}, u32[]{:S(2)}, u32[]{:S(2)}) %all-to-all-start) | async-done | bytes 524320 | tf_op jit(solution)/shard_map/all_to_all | solution.py:95
  15.7 0.9 copy.60
  16.6 0.2 slice_reduce_fusion.1
  16.9 33.9 %all-gather.2.cloned.1.call-done = bf16[512,1024]{1,0:T(8,128)(2,1)} async-done(((bf16[64,1024]{1,0:T(8,128)(2,1)}), bf16[512,1024]{1,0:T(8,128)(2,1)}) %all-gather.2.cloned.1.call-update) | async-done | bytes 1048592 | tf_op jit(solution)/shard_map/all_gather | solution.py:98
  50.8 2.3 %copy.46 = bf16[512,1024]{0,1:T(8,128)(2,1)} copy(bf16[512,1024]{1,0:T(8,128)(2,1)} %all-gather.2.cloned.1.call-done) | data formatting | bytes 2097152 | tf_op jit(solution)/shard_map/all_gather | solution.py:98
  53.1 1.6 %copy.48 = bf16[512,8,128]{2,0,1:T(8,128)(2,1)S(1)} copy(bf16[512,8,128]{0,2,1:T(8,128)(2,1)} %bitcast.121) | data formatting | bytes 2097152 | tf_op jit(solution)/shard_map/while/body/eval_jaxpr/while | solution.py:59
  54.7 7.4 %while.26 = (s32[]{:T(128)}, bf16[2,128,8]{1,2,0:T(8,128)(2,1)S(1)}, bf16[2,128,8]{1,2,0:T(8,128)(2,1)}, bf16[2,128,8,128]{3,1,2,0:T(8,128)(2,1)}, bf16[2,128,8,...) while((s32[]{:T(128)}, bf16[2,128,8]{1,2,0:T(8,128)(2,1)S(1)}, ...), condition=%wide.region_4.5_spmd, body=%wide.region_1.4_spmd.sunk | while | flops 272768000 | bytes 13944989 | solution.py:59
  54.7 1.0 %constant_dynamic-slice_fusion.2 = bf16[1,128,8,128]{3,2,1,0:T(8,128)(2,1)S(1)} fusion(bf16[2,128,8,128]{3,2,1,0:T(8,128)(2,1)} %get-tuple-element.220, s32[]{:T(128)S(6)} %copy.80), kind=kLoop, calls=%fused_computation.27.clone.1 | loop fusion | bytes 524292 | tf_op jit(solution)/shard_map/while/body/eval_jaxpr/while/body/jit(dynamic_index_in_dim)/dynamic_slice | solution.py:59
  55.7 0.0 copy-start.2
  55.7 0.5 bitcast_reduce_fusion.2
  56.2 0.6 fusion.37
  56.8 0.0 copy-done.2
  56.8 0.7 fusion.39
  57.6 0.0 copy-start.3
  57.6 0.7 fusion.38
  58.2 0.1 copy-done.3
  58.4 1.0 %constant_dynamic-slice_fusion.2 = bf16[1,128,8,128]{3,2,1,0:T(8,128)(2,1)S(1)} fusion(bf16[2,128,8,128]{3,2,1,0:T(8,128)(2,1)} %get-tuple-element.220, s32[]{:T(128)S(6)} %copy.80), kind=kLoop, calls=%fused_computation.27.clone.1 | loop fusion | bytes 524292 | tf_op jit(solution)/shard_map/while/body/eval_jaxpr/while/body/jit(dynamic_index_in_dim)/dynamic_slice | solution.py:59
  59.4 0.0 copy-start.2
  59.4 0.5 bitcast_reduce_fusion.2
  59.9 0.6 fusion.37
  60.5 0.7 fusion.39
  61.3 0.7 fusion.38
  61.9 0.1 copy-done.3
  62.1 1.9 %copy_bitcast_fusion.2 = bf16[2,128,1024]{2,1,0:T(8,128)(2,1)} fusion(bf16[2,128,8,128]{3,1,2,0:T(8,128)(2,1)} %get-tuple-element.95), kind=kLoop, calls=%fused_computation.34 | loop fusion | bytes 1048576 | tf_op jit(solution)/shard_map/convert_element_type | solution.py:104
  64.0 5.0 %all_to_all.20 = bf16[2,128,8]{1,2,0:T(8,128)(2,1)S(1)} all-to-all(bf16[2,128,8]{1,2,0:T(8,128)(2,1)S(1)} %get-tuple-element.94), channel_id=1, replica_groups=mesh['parts'=2,'shard'=2,'blk'=8] {'shard'}, dimensions={0} | all-to-all | bytes 8192 | tf_op jit(solution)/shard_map/all_to_all | solution.py:110
  69.0 3.5 %all-to-all-start.3 = ((bf16[2,128,8]{1,2,0:T(8,128)(2,1)}), bf16[2,128,8]{1,2,0:T(8,128)(2,1)S(1)}, u32[]{:S(2)}, u32[]{:S(2)}) async-start(bf16[2,128,8]{1,2,0:T(8,128)(2,1)} %get-tuple-element.96), calls=%async_computation.3 | async-start | bytes 8192 | tf_op jit(solution)/shard_map/all_to_all | solution.py:117
  72.5 0.1 copy.49
  72.7 0.9 all-to-all-done.3
  73.6 3.8 %all-to-all-start.2 = ((bf16[2,128,1024]{2,1,0:T(8,128)(2,1)}), bf16[2,128,1024]{2,1,0:T(8,128)(2,1)S(1)}, u32[]{:S(2)}, u32[]{:S(2)}) async-start(bf16[2,128,1024]{2,1,0:T(8,128)(2,1)} %copy_bitcast_fusion.2), calls=%async_computation.2 | async-start | bytes 1048576 | tf_op jit(solution)/shard_map/all_to_all | solution.py:103
  77.4 0.1 copy.54
  77.5 0.6 gather_fusion
  78.2 0.6 gather_fusion.4
  78.8 0.1 select_bitcast_fusion.5
  79.0 0.1 copy.55
  79.0 0.7 gather_fusion.1
  79.7 0.6 gather_fusion.5
  80.4 0.1 select_bitcast_fusion.4
  80.5 0.1 copy.56
  80.6 0.1 copy.57
  80.7 0.1 copy.52
  80.8 0.0 all-to-all-done.2
  80.9 0.1 convert_element_type.45
  81.0 0.1 slice_bitcast_fusion.1
  81.0 1.6 %gather_fusion.2 = f32[128,1024]{1,0:T(8,128)} fusion(f32[128,1024]{1,0:T(8,128)S(1)} %get-tuple-element.141, s32[1024]{0:T(1024)S(1)} %pad_clamp_fusion.1), kind=kCustom, calls=%fused_computation.1.clone | custom fusion | bytes 1049088 | tf_op jit(solution)/shard_map/jit(_take)/gather | solution.py:132
  82.6 1.1 %select_bitcast_fusion.1 = f32[16,8,8,128]{3,1,2,0:T(8,128)S(1)} fusion(f32[128,1024]{1,0:T(8,128)} %gather_fusion.2, pred[128]{0:T(512)(128)(4,1)S(1)} %get-tuple-element.156), kind=kLoop, calls=%fused_computation.38 | loop fusion | flops 131072 | bytes 1048704
  83.8 0.9 copy.61
  84.7 0.8 gather_fusion.3
  85.5 0.1 select_bitcast_fusion
  85.6 0.1 copy.62
  85.7 0.8 copy-done.1
  86.5 0.3 fusion.15
  86.8 0.2 divide_convert_fusion
  87.1 0.8 copy.70
  (25 shorter events, 0.3 us)
Async XLA Ops:
  6.5 1.9 %copy-start = (bf16[1024,1024]{1,0:T(8,128)(2,1)S(1)}, bf16[1024,1024]{1,0:T(8,128)(2,1)}, u32[]{:S(2)}) copy-start(bf16[1024,1024]{1,0:T(8,128)(2,1)} %param.11) | copy-start | bytes 6291460
  6.5 44.3 %all-gather.2.cloned.1.call-start = ((), (), s32[]{:S(2)}) async-start(), calls=%async_computation.4 | async-start | bytes 1179648 | tf_op jit(solution)/shard_map/all_gather | solution.py:98
  10.8 4.9 %all-to-all-start = ((bf16[2,128,1024]{2,1,0:T(8,128)(2,1)}), bf16[2,128,1024]{2,1,0:T(8,128)(2,1)S(1)}, u32[]{:S(2)}, u32[]{:S(2)}) async-start(bf16[2,128,1024]{2,1,0:T(8,128)(2,1)} %convolution_convert_fusion), calls=%async_computation | async-start | bytes 1048576 | tf_op jit(solution)/shard_map/all_to_all | solution.py:95
  55.7 1.1 %copy-start.2 = (bf16[2,128,8,128]{3,1,2,0:T(8,128)(2,1)S(1)}, bf16[2,128,8,128]{3,1,2,0:T(8,128)(2,1)}, u32[]{:S(2)}) copy-start(bf16[2,128,8,128]{3,1,2,0:T(8,128)(2,1)} %get-tuple-element.212) | copy-start | bytes 1572868 | tf_op jit(solution)/shard_map/while/body/eval_jaxpr/while
  57.6 0.8 copy-start.3
  59.4 1.1 %copy-start.2 = (bf16[2,128,8,128]{3,1,2,0:T(8,128)(2,1)S(1)}, bf16[2,128,8,128]{3,1,2,0:T(8,128)(2,1)}, u32[]{:S(2)}) copy-start(bf16[2,128,8,128]{3,1,2,0:T(8,128)(2,1)} %get-tuple-element.212) | copy-start | bytes 1572868 | tf_op jit(solution)/shard_map/while/body/eval_jaxpr/while
  61.3 0.8 copy-start.3
  69.0 4.6 %all-to-all-start.3 = ((bf16[2,128,8]{1,2,0:T(8,128)(2,1)}), bf16[2,128,8]{1,2,0:T(8,128)(2,1)S(1)}, u32[]{:S(2)}, u32[]{:S(2)}) async-start(bf16[2,128,8]{1,2,0:T(8,128)(2,1)} %get-tuple-element.96), calls=%async_computation.3 | async-start | bytes 8192 | tf_op jit(solution)/shard_map/all_to_all | solution.py:117
  73.6 7.3 %all-to-all-start.2 = ((bf16[2,128,1024]{2,1,0:T(8,128)(2,1)}), bf16[2,128,1024]{2,1,0:T(8,128)(2,1)S(1)}, u32[]{:S(2)}, u32[]{:S(2)}) async-start(bf16[2,128,1024]{2,1,0:T(8,128)(2,1)} %copy_bitcast_fusion.2), calls=%async_computation.2 | async-start | bytes 1048576 | tf_op jit(solution)/shard_map/all_to_all | solution.py:103
  85.5 1.0 %copy-start.1 = (f32[16,8,8,128]{3,2,1,0:T(8,128)S(1)}, f32[16,8,8,128]{3,2,1,0:T(8,128)}, u32[]{:S(2)}) copy-start(f32[16,8,8,128]{3,2,1,0:T(8,128)} %copy.61) | copy-start | bytes 1572868
Sparse Core Ops, SparseCore 0:
  9.5 41.2 all-gather.1
where the time goes:
time: 95.3 us; the launch traced here: 94.7 us
  waiting for transfers between devices  36.8 us (39%)
  local copies, waits for them, and re-layouts  18.4 us (19%)
  between operations  13.6 us (14%)
  starting transfers between devices  10.9 us (11%)
  blocking collectives  5.01 us (5%)
  matrix products  4.94 us (5%)
  other arithmetic  4.87 us (5%)
    all_gather x1, waiting for transfers between devices, local(): piece = lax.all_gather(bank, 'blk', axis=0, tiled=True)  33.9 us
    all_to_all x1, blocking collectives, local(): lax.all_to_all(top_part.reshape(2, item_count, HEADS).astype(jnp.bfloat16...  5.01 us
    unnamed x9, local copies, waits for them, and re-layouts  4.23 us
    all_to_all x1, starting transfers between devices, local(): lax.all_to_all(accum_part.reshape(2, item_count, width_all).astype(jnp.bf...  3.81 us
    all_to_all x1, starting transfers between devices, local(): lax.all_to_all(total_part.reshape(2, item_count, HEADS).astype(jnp.bfloat...  3.55 us
    all_to_all x1, starting transfers between devices, local(): lax.all_to_all(outgoing, 'shard', split_axis=0, concat_axis=0, tiled=True)  3.53 us
    dot_general x1, matrix products, local(): jnp.einsum('sct,td->scd', onehot_table.astype(jnp.bfloat16), projected, p...  2.43 us
    gather x2, local copies, waits for them, and re-layouts, local(): jnp.take(accum_back[member], safe_slot[:, member], axis=0)  2.38 us
  transfers between devices with their start and end apart: 4, of which 3 were waited for; matrix products, arithmetic and copies ran while one was open for 9% of the time, Pallas kernels for 0%

commit v1 on v0

--- a/solution.py
+++ b/solution.py
@@ -7,6 +7,24 @@
 HEADS = 8
 HEAD_DIM = 128
 NEGATIVE = -1e30
+
+
+def laid_out(pieces, dim):
+    lengths = list(pieces.shape[1:])
+    lengths[dim] *= pieces.shape[0]
+    return jnp.moveaxis(pieces, 0, dim).reshape(lengths)
+
+
+def collected_by_bits(shard, axis):
+    devices = lax.axis_size(axis)
+    parts = shard[None]
+    for level in range(devices.bit_length() - 1):
+        apart = 1 << level
+        received = lax.ppermute(parts, axis, [(i, i ^ apart) for i in range(devices)])
+        both = jnp.stack([parts, received])
+        upper = lax.axis_index(axis) >> level & 1
+        parts = jnp.where(upper == 0, both, both[::-1]).reshape(-1, *shard.shape)
+    return parts
 
 
 def empty_carry(slot_count):
@@ -95,7 +113,7 @@
     incoming = lax.all_to_all(outgoing, "shard", split_axis=0, concat_axis=0, tiled=True)
     item_count = incoming.shape[1]
     slot_heads = incoming.reshape(2 * item_count, HEADS, HEAD_DIM)
-    piece = lax.all_gather(bank, "blk", axis=0, tiled=True)
+    piece = laid_out(collected_by_bits(bank, "blk"), 0)
     allowed = jnp.ones((2 * item_count, piece.shape[0]), dtype=jnp.bool_)
     top_part, total_part, accum_part = fold_piece(
         empty_carry(2 * item_count), slot_heads, piece, allowed

time: 95.3 us -> 78.9 us (0.83)
  between operations: 13.6 us -> 0.28 us
  waiting for transfers between devices: 36.8 us -> 28.3 us
  starting transfers between devices: 10.9 us -> 17.6 us
  local copies, waits for them, and re-layouts: 18.4 us -> 15.6 us
  other arithmetic: 4.87 us -> 6.52 us
    all_gather x1 -> x0, waiting for transfers between devices: 33.9 us -> none  [local(): piece = lax.all_gather(bank, 'blk', axis=0, tiled=True)]
    ppermute x0 -> x3, waiting for transfers between devices: none -> 27.5 us  [collected_by_bits(): lax.ppermute(parts, axis, [(i, i ^ apart) for i in range(devices)])]
    ppermute x0 -> x3, starting transfers between devices: none -> 5.78 us  [collected_by_bits(): lax.ppermute(parts, axis, [(i, i ^ apart) for i in range(devices)])]
    all_gather x1 -> x0, local copies, waits for them, and re-layouts: 2.28 us -> none  [local(): piece = lax.all_gather(bank, 'blk', axis=0, tiled=True)]
    while x1, local copies, waits for them, and re-layouts: 1.61 us -> 0.14 us  [key_step(): lax.map(one_block, (blocked(query_heads), blocked(mask_all), blocked(top_...]
    another operation x3 -> x7, other arithmetic: 0.01 us -> 1.29 us  [the longest x4 1.28 us: collected_by_bits(): both = jnp.stack([parts, received])]
    all_to_all x1, waiting for transfers between devices: 1.28 us -> 0.01 us  [local(): lax.all_to_all(outgoing, 'shard', split_axis=0, concat_axis=0, tiled=True)]
    unnamed x9 -> x20, local copies, waits for them, and re-layouts: 4.23 us -> 4.57 us
  transfers between devices with their start and end apart: 4 -> 6, of which waited for: 3 -> 3; matrix products, arithmetic and copies ran while one was open for 9% -> 12% of each run, Pallas kernels for 0% -> 0%
where the time goes in v1:
time: 78.9 us; the launch traced here: 78.3 us
  waiting for transfers between devices  28.3 us (36%)
  starting transfers between devices  17.6 us (22%)
  local copies, waits for them, and re-layouts  15.6 us (20%)
  other arithmetic  6.52 us (8%)
  matrix products  4.95 us (6%)
  blocking collectives  4.89 us (6%)
    ppermute x3, waiting for transfers between devices, collected_by_bits(): lax.ppermute(parts, axis, [(i, i ^ apart) for i in range(devices)])  27.5 us
    ppermute x3, starting transfers between devices, collected_by_bits(): lax.ppermute(parts, axis, [(i, i ^ apart) for i in range(devices)])  5.78 us
    all_to_all x1, blocking collectives, local(): lax.all_to_all(top_part.reshape(2, item_count, HEADS).astype(jnp.bfloat16...  4.89 us
    unnamed x20, local copies, waits for them, and re-layouts  4.57 us
    all_to_all x1, starting transfers between devices, local(): lax.all_to_all(outgoing, 'shard', split_axis=0, concat_axis=0, tiled=True)  4.43 us
    all_to_all x1, starting transfers between devices, local(): lax.all_to_all(accum_part.reshape(2, item_count, width_all).astype(jnp.bf...  3.81 us
    all_to_all x1, starting transfers between devices, local(): lax.all_to_all(total_part.reshape(2, item_count, HEADS).astype(jnp.bfloat...  3.55 us
    dot_general x1, matrix products, local(): jnp.einsum('sct,td->scd', onehot_table.astype(jnp.bfloat16), projected, p...  2.43 us
  transfers between devices with their start and end apart: 6, of which 3 were waited for; matrix products, arithmetic and copies ran while one was open for 12% of the time, Pallas kernels for 0%

profile of v1, /device:TPU:1, one launch (start us, length us, event | category | flops | bytes accessed | tf_op | source)
XLA Modules:
  0.0 78.3 jit_solution(8117542033250080453)
XLA Ops:
  0.0 2.0 %collective-permute-start = (bf16[1,64,1024]{2,1,0:T(8,128)(2,1)}, bf16[1,64,1024]{2,1,0:T(8,128)(2,1)S(1)}, u32[]{:S(2)}, u32[]{:S(2)}) collective-permute-start(bf16[1,64,1024]{2,1,0:T(8,128)(2,1)} %bitcast.144), channel_id=1, source_target_pairs={{0,1},{1,0},{2,3},{3,2},{4,5},{5,4},{6,7},{7,6},{8,9},{9,8},{10,11... | collective-permute-start | bytes 393224 | tf_op jit(solution)/shard_map/ppermute | solution.py:23
  2.0 0.8 %copy.39 = s32[128,2]{1,0:T(8,128)S(1)} copy(s32[128,2]{0,1:T(2,128)} %param.13) | data formatting | bytes 2048 | tf_op args[3]
  2.8 0.1 copy.43
  2.9 0.2 reduce_window_sum.11
  3.1 0.1 copy.42
  3.2 2.4 %convolution_convert_fusion = bf16[2,128,1024]{2,1,0:T(8,128)(2,1)} fusion(bf16[128,1024]{1,0:T(8,128)(2,1)} %param.10, bf16[1024,1024]{1,0:T(8,128)(2,1)S(1)} %copy-done, s32[2,128]{1,0:T(2,128)S(1)} %copy.42, pred[2,128]{1,0:T(4,128)(4,1)S(1)} %copy.43), kind=kOutput, calls=%fused_computation.30 | convolution fusion | flops 336003072 | bytes 2884864 | tf_op jit(solution)/shard_map/sct,td->scd/dot_general | solution.py:107
  5.6 4.4 %all-to-all-start = ((bf16[2,128,1024]{2,1,0:T(8,128)(2,1)}), bf16[2,128,1024]{2,1,0:T(8,128)(2,1)S(1)}, u32[]{:S(2)}, u32[]{:S(2)}) async-start(bf16[2,128,1024]{2,1,0:T(8,128)(2,1)} %convolution_convert_fusion), calls=%async_computation | async-start | bytes 1048576 | tf_op jit(solution)/shard_map/all_to_all | solution.py:113
  10.1 0.0 collective-permute-done
  10.1 0.1 fusion.17
  10.2 1.4 %collective-permute-start.1 = (bf16[2,64,1024]{2,1,0:T(8,128)(2,1)S(1)}, bf16[2,64,1024]{2,1,0:T(8,128)(2,1)S(1)}, u32[]{:S(2)}, u32[]{:S(2)}) collective-permute-start(bf16[2,64,1024]{2,1,0:T(8,128)(2,1)S(1)} %get-tuple-element.144), channel_id=1, source_target_pairs={{0,2},{1,3},{2,0},{3,1},{4,6},{5,7},{6,4},{7,5},{8,10},{9,11},{10,... | collective-permute-start | bytes 786440 | tf_op jit(solution)/shard_map/ppermute | solution.py:23
  11.5 0.7 slice_reduce_fusion.1
  12.3 5.8 %collective-permute-done.1 = bf16[2,64,1024]{2,1,0:T(8,128)(2,1)S(1)} collective-permute-done((bf16[2,64,1024]{2,1,0:T(8,128)(2,1)S(1)}, bf16[2,64,1024]{2,1,0:T(8,128)(2,1)S(1)}, u32[]{:S(2)}, u32[]{:S(2)}) %collective-permute-start.1) | collective-permute-done | bytes 262176 | tf_op jit(solution)/shard_map/ppermute | solution.py:23
  18.1 0.1 pad_maximum_fusion.1
  18.2 0.1 reverse_select_fusion.1
  18.3 2.4 %collective-permute-start.2 = (bf16[4,64,1024]{2,1,0:T(8,128)(2,1)S(1)}, bf16[4,64,1024]{2,1,0:T(8,128)(2,1)}, u32[]{:S(2)}, u32[]{:S(2)}) collective-permute-start(bf16[4,64,1024]{2,1,0:T(8,128)(2,1)S(1)} %bitcast.140), channel_id=1, source_target_pairs={{0,4},{1,5},{2,6},{3,7},{4,0},{5,1},{6,2},{7,3},{8,12},{9,13},{10,... | collective-permute-start | bytes 1572872 | tf_op jit(solution)/shard_map/ppermute | solution.py:23
  20.7 0.1 copy.40
  20.8 0.9 %copy.57 = bf16[32,8,8,128]{3,2,1,0:T(8,128)(2,1)} copy(bf16[32,8,8,128]{3,1,2,0:T(8,128)(2,1)S(1)} %bitcast.137) | data formatting | bytes 1048576
  21.8 21.6 %collective-permute-done.2 = bf16[4,64,1024]{2,1,0:T(8,128)(2,1)} collective-permute-done((bf16[4,64,1024]{2,1,0:T(8,128)(2,1)S(1)}, bf16[4,64,1024]{2,1,0:T(8,128)(2,1)}, u32[]{:S(2)}, u32[]{:S(2)}) %collective-permute-start.2) | collective-permute-done | bytes 524320 | tf_op jit(solution)/shard_map/ppermute | solution.py:23
  43.4 1.1 %pad_maximum_fusion = bf16[2,4,64,1024]{3,2,1,0:T(8,128)(2,1)S(1)} fusion(bf16[1,4,64,1024]{3,2,1,0:T(8,128)(2,1)} %bitcast.17, bf16[1,4,64,1024]{3,2,1,0:T(8,128)(2,1)S(1)} %bitcast.141), kind=kLoop, calls=%fused_computation.33 | loop fusion | flops 524288 | bytes 2097152 | tf_op jit(solution)/shard_map/stack | solution.py:24
  44.5 0.3 reverse_select_fusion
  44.8 0.3 copy.58
  45.1 0.1 copy.45
  45.2 7.4 %while.26 = (s32[]{:T(128)}, bf16[2,128,8]{1,2,0:T(8,128)(2,1)S(1)}, bf16[2,128,8]{1,2,0:T(8,128)(2,1)}, bf16[2,128,8,128]{3,1,2,0:T(8,128)(2,1)}, bf16[2,128,8,...) while((s32[]{:T(128)}, bf16[2,128,8]{1,2,0:T(8,128)(2,1)S(1)}, ...), condition=%wide.region_4.5_spmd, body=%wide.region_1.4_spmd.sunk | while | flops 272768000 | bytes 13944989 | solution.py:77
  45.3 1.0 %constant_dynamic-slice_fusion.2 = bf16[1,128,8,128]{3,2,1,0:T(8,128)(2,1)S(1)} fusion(bf16[2,128,8,128]{3,2,1,0:T(8,128)(2,1)} %get-tuple-element.222, s32[]{:T(128)S(6)} %copy.78), kind=kLoop, calls=%fused_computation.27.clone.1 | loop fusion | bytes 524292 | tf_op jit(solution)/shard_map/while/body/eval_jaxpr/while/body/jit(dynamic_index_in_dim)/dynamic_slice | solution.py:77
  46.2 0.5 bitcast_reduce_fusion.2
  46.8 0.6 fusion.39
  47.4 0.7 fusion.41
  48.1 0.6 fusion.40
  48.8 0.2 copy-done.3
  48.9 1.0 %constant_dynamic-slice_fusion.2 = bf16[1,128,8,128]{3,2,1,0:T(8,128)(2,1)S(1)} fusion(bf16[2,128,8,128]{3,2,1,0:T(8,128)(2,1)} %get-tuple-element.222, s32[]{:T(128)S(6)} %copy.78), kind=kLoop, calls=%fused_computation.27.clone.1 | loop fusion | bytes 524292 | tf_op jit(solution)/shard_map/while/body/eval_jaxpr/while/body/jit(dynamic_index_in_dim)/dynamic_slice | solution.py:77
  49.9 0.5 bitcast_reduce_fusion.2
  50.5 0.6 fusion.39
  51.1 0.7 fusion.41
  51.8 0.6 fusion.40
  52.5 0.2 copy-done.3
  52.6 1.9 %copy_bitcast_fusion.2 = bf16[2,128,1024]{2,1,0:T(8,128)(2,1)} fusion(bf16[2,128,8,128]{3,1,2,0:T(8,128)(2,1)} %get-tuple-element.95), kind=kLoop, calls=%fused_computation.37 | loop fusion | bytes 1048576 | tf_op jit(solution)/shard_map/convert_element_type | solution.py:122
  54.5 4.9 %all_to_all.20 = bf16[2,128,8]{1,2,0:T(8,128)(2,1)S(1)} all-to-all(bf16[2,128,8]{1,2,0:T(8,128)(2,1)S(1)} %get-tuple-element.94), channel_id=1, replica_groups=mesh['parts'=2,'shard'=2,'blk'=8] {'shard'}, dimensions={0} | all-to-all | bytes 8192 | tf_op jit(solution)/shard_map/all_to_all | solution.py:128
  59.4 3.5 %all-to-all-start.3 = ((bf16[2,128,8]{1,2,0:T(8,128)(2,1)}), bf16[2,128,8]{1,2,0:T(8,128)(2,1)S(1)}, u32[]{:S(2)}, u32[]{:S(2)}) async-start(bf16[2,128,8]{1,2,0:T(8,128)(2,1)} %get-tuple-element.96), calls=%async_computation.3 | async-start | bytes 8192 | tf_op jit(solution)/shard_map/all_to_all | solution.py:135
  63.0 0.1 copy.46
  63.1 0.9 %all-to-all-done.3 = bf16[2,128,8]{1,2,0:T(8,128)(2,1)S(1)} async-done(((bf16[2,128,8]{1,2,0:T(8,128)(2,1)}), bf16[2,128,8]{1,2,0:T(8,128)(2,1)S(1)}, u32[]{:S(2)}, u32[]{:S(2)}) %all-to-all-start.3) | async-done | bytes 4128 | tf_op jit(solution)/shard_map/all_to_all | solution.py:135
  64.0 3.8 %all-to-all-start.2 = ((bf16[2,128,1024]{2,1,0:T(8,128)(2,1)}), bf16[2,128,1024]{2,1,0:T(8,128)(2,1)S(1)}, u32[]{:S(2)}, u32[]{:S(2)}) async-start(bf16[2,128,1024]{2,1,0:T(8,128)(2,1)} %copy_bitcast_fusion.2), calls=%async_computation.2 | async-start | bytes 1048576 | tf_op jit(solution)/shard_map/all_to_all | solution.py:121
  67.8 0.1 copy.51
  68.0 0.6 gather_fusion
  68.6 0.6 gather_fusion.4
  69.3 0.1 select_bitcast_fusion.5
  69.4 0.1 copy.52
  69.5 0.7 gather_fusion.1
  70.1 0.6 gather_fusion.5
  70.8 0.1 select_bitcast_fusion.4
  70.9 0.1 copy.53
  71.0 0.1 copy.54
  71.1 0.1 copy.49
  71.3 0.1 convert_element_type.45
  71.4 0.1 slice_bitcast_fusion.1
  71.5 1.6 %gather_fusion.2 = f32[128,1024]{1,0:T(8,128)} fusion(f32[128,1024]{1,0:T(8,128)S(1)} %get-tuple-element.141, s32[1024]{0:T(1024)S(1)} %pad_clamp_fusion.1), kind=kCustom, calls=%fused_computation.1.clone | custom fusion | bytes 1049088 | tf_op jit(solution)/shard_map/jit(_take)/gather | solution.py:150
  73.1 1.1 %select_bitcast_fusion.1 = f32[16,8,8,128]{3,1,2,0:T(8,128)S(1)} fusion(f32[128,1024]{1,0:T(8,128)} %gather_fusion.2, pred[128]{0:T(512)(128)(4,1)S(1)} %get-tuple-element.158), kind=kLoop, calls=%fused_computation.42 | loop fusion | flops 131072 | bytes 1048704
  74.2 0.9 %copy.59 = f32[16,8,8,128]{3,2,1,0:T(8,128)} copy(f32[16,8,8,128]{3,1,2,0:T(8,128)S(1)} %select_bitcast_fusion.1) | data formatting | bytes 1048576
  75.1 0.8 %gather_fusion.3 = f32[128,1024]{1,0:T(8,128)S(1)} fusion(f32[128,1024]{1,0:T(8,128)S(1)} %get-tuple-element.142, s32[1024]{0:T(1024)S(1)} %pad_clamp_fusion), kind=kCustom, calls=%fused_computation.5.clone | custom fusion | bytes 1049088 | tf_op jit(solution)/shard_map/jit(_take)/gather | solution.py:150
  75.9 0.1 select_bitcast_fusion
  76.0 0.1 copy.60
  76.1 0.8 %copy-done.1 = f32[16,8,8,128]{3,2,1,0:T(8,128)S(1)} copy-done((f32[16,8,8,128]{3,2,1,0:T(8,128)S(1)}, f32[16,8,8,128]{3,2,1,0:T(8,128)}, u32[]{:S(2)}) %copy-start.1) | copy-done | bytes 524312
  77.0 0.3 fusion.15
  77.3 0.2 divide_convert_fusion
  77.5 0.8 copy.68
  (44 shorter events, 0.4 us)
Async XLA Ops:
  0.0 3.2 %copy-start = (bf16[1024,1024]{1,0:T(8,128)(2,1)S(1)}, bf16[1024,1024]{1,0:T(8,128)(2,1)}, u32[]{:S(2)}) copy-start(bf16[1024,1024]{1,0:T(8,128)(2,1)} %param.11) | copy-start | bytes 6291460
  0.0 10.1 %collective-permute-start = (bf16[1,64,1024]{2,1,0:T(8,128)(2,1)}, bf16[1,64,1024]{2,1,0:T(8,128)(2,1)S(1)}, u32[]{:S(2)}, u32[]{:S(2)}) collective-permute-start(bf16[1,64,1024]{2,1,0:T(8,128)(2,1)} %bitcast.144), channel_id=1, source_target_pairs={{0,1},{1,0},{2,3},{3,2},{4,5},{5,4},{6,7},{7,6},{8,9},{9,8},{10,11... | collective-permute-start | bytes 393224 | tf_op jit(solution)/shard_map/ppermute | solution.py:23
  3.1 7.0 %copy-start.4 = (bf16[64,1024]{1,0:T(8,128)(2,1)S(1)}, bf16[64,1024]{1,0:T(8,128)(2,1)}, u32[]{:S(2)}) copy-start(bf16[64,1024]{1,0:T(8,128)(2,1)} %param.12) | copy-start | bytes 393220
  5.6 15.2 %all-to-all-start = ((bf16[2,128,1024]{2,1,0:T(8,128)(2,1)}), bf16[2,128,1024]{2,1,0:T(8,128)(2,1)S(1)}, u32[]{:S(2)}, u32[]{:S(2)}) async-start(bf16[2,128,1024]{2,1,0:T(8,128)(2,1)} %convolution_convert_fusion), calls=%async_computation | async-start | bytes 1048576 | tf_op jit(solution)/shard_map/all_to_all | solution.py:113
  10.2 8.0 %collective-permute-start.1 = (bf16[2,64,1024]{2,1,0:T(8,128)(2,1)S(1)}, bf16[2,64,1024]{2,1,0:T(8,128)(2,1)S(1)}, u32[]{:S(2)}, u32[]{:S(2)}) collective-permute-start(bf16[2,64,1024]{2,1,0:T(8,128)(2,1)S(1)} %get-tuple-element.144), channel_id=1, source_target_pairs={{0,2},{1,3},{2,0},{3,1},{4,6},{5,7},{6,4},{7,5},{8,10},{9,11},{10,... | collective-permute-start | bytes 786440 | tf_op jit(solution)/shard_map/ppermute | solution.py:23
  12.3 8.4 %copy-start.5 = (s32[128]{0:T(128)S(1)}, s32[128]{0:T(128)}, u32[]{:S(2)}) copy-start(s32[128]{0:T(128)} %get-tuple-element.121) | copy-start | bytes 1540
  12.3 8.4 %copy-start.7 = (s32[128]{0:T(128)S(1)}, s32[128]{0:T(128)}, u32[]{:S(2)}) copy-start(s32[128]{0:T(128)} %get-tuple-element.122) | copy-start | bytes 1540
  18.1 3.6 %copy-start.6 = (s32[128]{0:T(128)S(1)}, s32[128]{0:T(128)}, u32[]{:S(2)}) copy-start(s32[128]{0:T(128)} %get-tuple-element.121) | copy-start | bytes 1540
  18.1 3.6 %copy-start.8 = (s32[128]{0:T(128)S(1)}, s32[128]{0:T(128)}, u32[]{:S(2)}) copy-start(s32[128]{0:T(128)} %get-tuple-element.122) | copy-start | bytes 1540
  18.3 25.1 %collective-permute-start.2 = (bf16[4,64,1024]{2,1,0:T(8,128)(2,1)S(1)}, bf16[4,64,1024]{2,1,0:T(8,128)(2,1)}, u32[]{:S(2)}, u32[]{:S(2)}) collective-permute-start(bf16[4,64,1024]{2,1,0:T(8,128)(2,1)S(1)} %bitcast.140), channel_id=1, source_target_pairs={{0,4},{1,5},{2,6},{3,7},{4,0},{5,1},{6,2},{7,3},{8,12},{9,13},{10,... | collective-permute-start | bytes 1572872 | tf_op jit(solution)/shard_map/ppermute | solution.py:23
  46.2 1.1 %copy-start.2 = (bf16[2,128,8,128]{3,1,2,0:T(8,128)(2,1)S(1)}, bf16[2,128,8,128]{3,1,2,0:T(8,128)(2,1)}, u32[]{:S(2)}) copy-start(bf16[2,128,8,128]{3,1,2,0:T(8,128)(2,1)} %get-tuple-element.214) | copy-start | bytes 1572868 | tf_op jit(solution)/shard_map/while/body/eval_jaxpr/while
  48.1 0.8 %copy-start.3 = (bf16[2,128,8,128]{3,1,2,0:T(8,128)(2,1)}, bf16[2,128,8,128]{3,1,2,0:T(8,128)(2,1)S(1)}, u32[]{:S(2)}) copy-start(bf16[2,128,8,128]{3,1,2,0:T(8,128)(2,1)S(1)} %fusion.41) | copy-start | bytes 1572868 | tf_op jit(solution)/shard_map/while/body/eval_jaxpr/while
  49.9 1.1 %copy-start.2 = (bf16[2,128,8,128]{3,1,2,0:T(8,128)(2,1)S(1)}, bf16[2,128,8,128]{3,1,2,0:T(8,128)(2,1)}, u32[]{:S(2)}) copy-start(bf16[2,128,8,128]{3,1,2,0:T(8,128)(2,1)} %get-tuple-element.214) | copy-start | bytes 1572868 | tf_op jit(solution)/shard_map/while/body/eval_jaxpr/while
  51.8 0.8 %copy-start.3 = (bf16[2,128,8,128]{3,1,2,0:T(8,128)(2,1)}, bf16[2,128,8,128]{3,1,2,0:T(8,128)(2,1)S(1)}, u32[]{:S(2)}) copy-start(bf16[2,128,8,128]{3,1,2,0:T(8,128)(2,1)S(1)} %fusion.41) | copy-start | bytes 1572868 | tf_op jit(solution)/shard_map/while/body/eval_jaxpr/while
  59.4 4.6 %all-to-all-start.3 = ((bf16[2,128,8]{1,2,0:T(8,128)(2,1)}), bf16[2,128,8]{1,2,0:T(8,128)(2,1)S(1)}, u32[]{:S(2)}, u32[]{:S(2)}) async-start(bf16[2,128,8]{1,2,0:T(8,128)(2,1)} %get-tuple-element.96), calls=%async_computation.3 | async-start | bytes 8192 | tf_op jit(solution)/shard_map/all_to_all | solution.py:135
  64.0 7.3 %all-to-all-start.2 = ((bf16[2,128,1024]{2,1,0:T(8,128)(2,1)}), bf16[2,128,1024]{2,1,0:T(8,128)(2,1)S(1)}, u32[]{:S(2)}, u32[]{:S(2)}) async-start(bf16[2,128,1024]{2,1,0:T(8,128)(2,1)} %copy_bitcast_fusion.2), calls=%async_computation.2 | async-start | bytes 1048576 | tf_op jit(solution)/shard_map/all_to_all | solution.py:121
  75.9 1.0 %copy-start.1 = (f32[16,8,8,128]{3,2,1,0:T(8,128)S(1)}, f32[16,8,8,128]{3,2,1,0:T(8,128)}, u32[]{:S(2)}) copy-start(f32[16,8,8,128]{3,2,1,0:T(8,128)} %copy.59) | copy-start | bytes 1572868
